TPU v7x, 128 devices: a whole 4x4x4 slice. The times are simulated.
128 devices in a mesh: cube: 128 (over x, y, z, core).
Axes of the slice: x: 4, y: 4, z: 4, core: 2. Of those that a mesh axis runs over, the one named last changes fastest.
Arguments:
- vectors: bfloat16 [524288, 768], P('cube'), may hold values from -40 to 40
- child_labels: int32 [2, 524288], P(None, 'cube'), may hold values from 0 to 1, as said below
Outputs:
- held: bfloat16 [917504, 768], P('cube')
- margin_one: float32 [786432], P('cube')
- margin_two: float32 [917504], P('cube')
- centroids: float32 [6, 768], replicated
Inputs may be any that keep to these rules, and one draw needn't show every extreme that they name: `child_labels`: per device, the vectors leaving at the first level number from 1024 to 2048, and 2048 on some device in every draw. `child_labels`: per device, the second-level leavers among its vectors that stay at the first level number at most 512, and among the vectors it sends away at the first level at most 512; in every draw some device holds 512 second-level leavers of each kind (its own stayers and those received at the first level), so its second-level send buffer is full.
All inputs are finite; a program needn't handle non-finite values.
Results may differ from a plain program's by a relative error of at most 0.0011.
Values may be sent and summed in bfloat16 or wider, within the bound.
A program may use at most 128 MiB of HBM per device.

v0:
```python
import jax
import jax.numpy as jnp
from jax import lax
from jax.sharding import PartitionSpec as P


def from_partner(shard, axis, stride):
    return lax.ppermute(shard, axis, [(i, i ^ 1 << stride) for i in range(lax.axis_size(axis))])


def shortened(shard):

    def short(part):
        return part.astype(jnp.bfloat16) if part.dtype == jnp.float32 else part

    return jax.tree.map(short, shard)


def compact(mask, rows, cap, fill):
    place = jnp.cumsum(mask.astype(jnp.int32)) - 1
    index = jnp.where(mask, place, cap)
    base = jnp.full((cap + 1,) + rows.shape[1:], fill, rows.dtype)
    return base.at[index].set(rows)[:cap]


def split_margin(held_rows, live, pair, width):
    scores = jnp.dot(held_rows, pair.astype(jnp.bfloat16).T, preferred_element_type=jnp.float32)
    offset = 0.5 * (jnp.sum(pair[1] * pair[1]) - jnp.sum(pair[0] * pair[0]))
    return jnp.where(live, (scores[:, 1] - scores[:, 0] - offset) / width, jnp.float32(0.0))


def local(vectors, child_labels):
    ways = lax.axis_size("cube")
    levels = ways.bit_length() - 1
    top_bit = levels - 1
    next_bit = levels - 2
    here = lax.axis_index("cube")
    bit_one = here >> top_bit & 1
    bit_two = here >> next_bit & 1
    rows, width = vectors.shape
    cap_one = rows // 2
    cap_two = rows // 4
    first = child_labels[0]
    later = child_labels[1]
    leave = first != bit_one
    stay = jnp.logical_not(leave)
    send_rows = compact(leave, vectors, cap_one, 0)
    send_tags = compact(leave, later, cap_one, -1)
    got_rows, got_tags = from_partner((send_rows, send_tags), "cube", top_bit)
    held_one = jnp.concatenate(
        [jnp.where(stay[:, None], vectors, jnp.zeros((), jnp.bfloat16)), got_rows], axis=0
    )
    tags = jnp.concatenate([jnp.where(stay, later, -1), got_tags], axis=0)
    live_one = tags >= 0
    slot_one = (jnp.arange(2) == bit_one).astype(jnp.float32)
    part_one = slot_one[:, None] * jnp.sum(held_one, axis=0, dtype=jnp.float32)[None]
    tally_one = slot_one * jnp.sum(live_one).astype(jnp.float32)
    total_one, number_one = lax.psum((part_one, tally_one), "cube")
    centre_one = total_one / number_one[:, None]
    margin_one = split_margin(held_one, live_one, centre_one, width)
    moving = live_one & (tags != bit_two)
    out_rows = compact(moving, held_one, cap_two, 0)
    out_tags = compact(moving, tags, cap_two, -1)
    in_rows, in_tags = (
        from_partner(out_rows, "cube", next_bit),
        from_partner(shortened(out_tags), "cube", next_bit).astype(out_tags.dtype),
    )
    held_two = jnp.concatenate(
        [jnp.where(moving[:, None], jnp.zeros((), jnp.bfloat16), held_one), in_rows], axis=0
    )
    live_two = jnp.concatenate([live_one & jnp.logical_not(moving), in_tags >= 0], axis=0)
    slot_two = (jnp.arange(4) == 2 * bit_one + bit_two).astype(jnp.float32)
    part_two = slot_two[:, None] * jnp.sum(held_two, axis=0, dtype=jnp.float32)[None]
    tally_two = slot_two * jnp.sum(live_two).astype(jnp.float32)
    total_two, number_two = lax.psum((part_two, tally_two), "cube")
    centre_two = total_two / number_two[:, None]
    pair = lax.dynamic_slice_in_dim(centre_two, 2 * bit_one, 2, 0)
    margin_two = split_margin(held_two, live_two, pair, width)
    centroids = jnp.concatenate([centre_one, centre_two], axis=0)
    return (held_two, margin_one, margin_two, centroids)


def solution(mesh):
    return jax.shard_map(
        local,
        mesh=mesh,
        in_specs=(P("cube", None), P(None, "cube")),
        out_specs=(P("cube", None), P("cube"), P("cube"), P()),
        check_vma=False,
    )
```

profile of v0, /device:TPU:1, one launch (start us, length us, event | category | flops | bytes accessed | tf_op | source)
XLA Modules:
  0.0 282.3 jit_solution(13088626194844371804)
XLA Ops:
  0.6 0.8 slice.61
  1.4 0.8 fusion.21
  2.2 0.3 reduce-window.16
  2.5 0.1 slice.78
  2.6 0.1 reduce-window.19
  2.7 0.1 slice_reduce_fusion.1
  2.8 0.1 add_add_fusion.1
  2.8 0.8 compare_select_fusion.1
  3.6 15.5 %scatter_custom_fusion = s32[2049]{0:T(1024)S(1)} fusion(s32[4096]{0:T(1024)S(1)} %bitcast.34, s32[4096]{0:T(1024)S(1)} %bitcast.30, s32[]{:T(128)} %constant.19.clone.1), kind=kCustom, calls=%fused_computation.44 | custom fusion | bytes 8200 | tf_op jit(solution)/shard_map/scatter | solution.py:23
  19.2 3.7 %collective-permute-start = (s32[2048]{0:T(1024)S(1)}, s32[2048]{0:T(1024)S(1)}, u32[]{:S(2)}, u32[]{:S(2)}) collective-permute-start(s32[2048]{0:T(1024)S(1)} %slice.80), channel_id=1, source_target_pairs={{0,64},{1,65},{2,66},{3,67},{4,68},{5,69},{6,70},{7,71},{8,72},{9,... | collective-permute-start | bytes 24584 | tf_op jit(solution)/shard_map/ppermute | solution.py:8
  22.8 20.0 %scatter_custom_fusion.1 = bf16[2049,768]{1,0:T(8,128)(2,1)S(1)} fusion(s32[4096]{0:T(1024)S(1)} %bitcast.35, bf16[4096,768]{1,0:T(8,128)(2,1)} %param.2, bf16[]{:T(256)} %constant.24.clone.1), kind=kCustom, calls=%fused_computation.10 | custom fusion | bytes 3147776 | tf_op jit(solution)/shard_map/scatter | solution.py:23
  42.9 0.0 copy-start
  42.9 1.9 slice.81
  44.7 0.0 collective-permute-start.1
  44.8 2.0 copy-done
  46.8 4.1 %broadcast_select_fusion.1 = bf16[4096,768]{1,0:T(8,128)(2,1)} fusion(bf16[4096,768]{1,0:T(8,128)(2,1)S(1)} %copy-done, pred[4096]{0:T(1024)(128)(4,1)S(1)} %not.10), kind=kLoop, calls=%fused_computation.9 | loop fusion | flops 3145728 | bytes 12587008 | tf_op jit(solution)/shard_map/jit(_where)/select_n | solution.py:51
  50.9 0.6 convert_reduce_fusion.3
  52.2 0.3 reduce-window.24
  52.5 0.1 slice.82
  52.6 0.1 reduce-window.25
  52.7 0.1 slice_reduce_fusion
  52.8 0.1 add_add_fusion
  52.9 0.1 compare_select_fusion
  52.9 23.0 %scatter_custom_fusion.3 = s32[1025]{0:T(1024)S(1)} fusion(s32[6144]{0:T(1024)S(1)} %bitcast.32, s32[6144]{0:T(1024)S(1)} %pad_add_fusion.1, s32[]{:T(128)} %constant.19.clone.1), kind=kCustom, calls=%fused_computation.46 | custom fusion | bytes 4104 | tf_op jit(solution)/shard_map/scatter | solution.py:23
  75.9 0.4 collective-permute-start.3
  76.3 37.5 %collective-permute-done.3 = s32[1024]{0:T(1024)S(1)} collective-permute-done((s32[1024]{0:T(1024)S(1)}, s32[1024]{0:T(1024)S(1)}, u32[]{:S(2)}, u32[]{:S(2)}) %collective-permute-start.3) | collective-permute-done | bytes 4128 | tf_op jit(solution)/shard_map/ppermute | solution.py:8
  113.8 0.6 convert_reduce_fusion.2
  115.1 0.1 collective-permute-done.1
  115.2 31.5 %scatter_custom_fusion.2 = bf16[1025,768]{1,0:T(8,128)(2,1)} fusion(s32[6144]{0:T(1024)S(1)} %bitcast.33, bf16[]{:T(256)} %constant.24.clone.1, bf16[2048,768]{1,0:T(8,128)(2,1)} %collective-permute-done.1, bf16[4096,768]{1,0:T(8,128)(2,1)} %broadcast_select_fusion.1), kind=kCustom, calls=%fused_computation.12 | custom fusion | flops 18874368 | bytes 11011586 | tf_op jit(solution)/shard_map/scatter | solution.py:23
  146.8 2.8 %slice.84 = bf16[1024,768]{1,0:T(8,128)(2,1)} slice(bf16[1025,768]{1,0:T(8,128)(2,1)} %scatter_custom_fusion.2), slice={[0:1024], [0:768]} | slice | bytes 3145728 | tf_op jit(solution)/shard_map/slice | solution.py:23
  149.6 0.1 collective-permute-start.2
  149.7 5.1 %convert_reduce_fusion.1 = f32[768]{0:T(1024)S(1)} fusion(bf16[2048,768]{1,0:T(8,128)(2,1)} %collective-permute-done.1, bf16[4096,768]{1,0:T(8,128)(2,1)} %broadcast_select_fusion.1), kind=kLoop, calls=%fused_computation.5 | loop fusion | flops 23592192 | bytes 9440256 | tf_op jit(solution)/shard_map/reduce_sum | solution.py:56
  154.8 0.1 broadcast_multiply_fusion.1
  154.9 7.0 %broadcast_select_fusion = bf16[6144,768]{1,0:T(8,128)(2,1)S(1)} fusion(pred[6144]{0:T(1024)(128)(4,1)S(1)} %get-tuple-element.13, bf16[2048,768]{1,0:T(8,128)(2,1)} %collective-permute-done.1, bf16[4096,768]{1,0:T(8,128)(2,1)S(1)} %bitcast.22), kind=kLoop, calls=%fused_computation.8 | loop fusion | flops 23592960 | bytes 18880512 | tf_op jit(solution)/shard_map/jit(_where)/select_n | solution.py:69
  161.9 22.0 %collective-permute-done.2 = bf16[1024,768]{1,0:T(8,128)(2,1)} collective-permute-done((bf16[1024,768]{1,0:T(8,128)(2,1)}, bf16[1024,768]{1,0:T(8,128)(2,1)}, u32[]{:S(2)}, u32[]{:S(2)}) %collective-permute-start.2) | collective-permute-done | bytes 1572896 | tf_op jit(solution)/shard_map/ppermute | solution.py:8
  183.9 11.5 %convert_reduce_fusion = (f32[768]{0:T(1024)S(1)}, bf16[7168,768]{1,0:T(8,128)(2,1)}) fusion(bf16[1024,768]{1,0:T(8,128)(2,1)} %collective-permute-done.2, bf16[6144,768]{1,0:T(8,128)(2,1)S(1)} %broadcast_select_fusion), kind=kLoop, calls=%fused_computation.4 | loop fusion | flops 33029376 | bytes 22023168 | tf_op jit(solution)/shard_map/reduce_sum | solution.py:73
  195.5 0.1 broadcast_multiply_fusion
  195.5 68.5 %all-reduce = (f32[2,768]{1,0:T(2,128)S(1)}, f32[2]{0:T(128)S(1)}, f32[4,768]{1,0:T(4,128)S(1)}, f32[4]{0:T(128)S(1)}) all-reduce(f32[2,768]{1,0:T(2,128)S(1)} %broadcast_multiply_fusion.1, f32[2]{0:T(128)S(1)} %compare_select_fusion.3, f32[4,768]{1,0:T(4,128)S(1)} %broadcast_multiply_fusion, ...), channel_id=1, replica_groups=mesh['cube'=128] {'cube'}, use_global_device_ids=true, to_apply=%region_8.9 | all-reduce | flops 4614 | bytes 36912 | tf_op jit(solution)/shard_map/psum | solution.py:58
  264.1 0.1 broadcast_divide_fusion.1
  264.1 0.6 fusion.16
  266.0 5.1 %fusion.13 = f32[6144,2]{0,1:T(2,128)S(1)} fusion(f32[2,768]{1,0:T(2,128)S(1)} %broadcast_divide_fusion.1, bf16[2048,768]{1,0:T(8,128)(2,1)} %collective-permute-done.1, bf16[4096,768]{1,0:T(8,128)(2,1)} %broadcast_select_fusion.1), kind=kOutput, calls=%fused_computation.54 | convolution fusion | flops 37750272 | bytes 9492480 | tf_op jit(solution)/shard_map/dot_general | solution.py:27
  271.2 0.6 broadcast_select_fusion.3
  271.8 0.1 broadcast_divide_fusion
  271.9 0.6 pad_maximum_fusion.2
  272.5 0.7 fusion.18
  274.6 7.1 %fusion.12 = f32[7168,2]{0,1:T(2,128)S(1)} fusion(bf16[7168,768]{1,0:T(8,128)(2,1)} %get-tuple-element.16, f32[4,768]{1,0:T(4,128)S(1)} %broadcast_divide_fusion, s32[]{:T(128)S(6)} %select_n.85), kind=kOutput, calls=%fused_computation.49 | convolution fusion | flops 22020096 | bytes 11070468 | tf_op jit(solution)/shard_map/dot_general | solution.py:27
  281.6 0.1 fusion.5
  281.7 0.6 broadcast_select_fusion.2
  (19 shorter events, 0.1 us)
Async XLA Ops:
  19.2 31.7 %collective-permute-start = (s32[2048]{0:T(1024)S(1)}, s32[2048]{0:T(1024)S(1)}, u32[]{:S(2)}, u32[]{:S(2)}) collective-permute-start(s32[2048]{0:T(1024)S(1)} %slice.80), channel_id=1, source_target_pairs={{0,64},{1,65},{2,66},{3,67},{4,68},{5,69},{6,70},{7,71},{8,72},{9,... | collective-permute-start | bytes 24584 | tf_op jit(solution)/shard_map/ppermute | solution.py:8
  42.9 3.9 %copy-start = (bf16[4096,768]{1,0:T(8,128)(2,1)S(1)}, bf16[4096,768]{1,0:T(8,128)(2,1)}, u32[]{:S(2)}) copy-start(bf16[4096,768]{1,0:T(8,128)(2,1)} %param.2) | copy-start | bytes 18874372
  44.7 70.5 %collective-permute-start.1 = (bf16[2048,768]{1,0:T(8,128)(2,1)}, bf16[2048,768]{1,0:T(8,128)(2,1)}, u32[]{:S(2)}, u32[]{:S(2)}) collective-permute-start(bf16[2048,768]{1,0:T(8,128)(2,1)} %slice.81), channel_id=1, source_target_pairs={{0,64},{1,65},{2,66},{3,67},{4,68},{5,69},{6,70},{7,71},{8,72},{9,... | collective-permute-start | bytes 9437192 | tf_op jit(solution)/shard_map/ppermute | solution.py:8
  75.9 37.8 %collective-permute-start.3 = (s32[1024]{0:T(1024)S(1)}, s32[1024]{0:T(1024)S(1)}, u32[]{:S(2)}, u32[]{:S(2)}) collective-permute-start(s32[1024]{0:T(1024)S(1)} %slice.89), channel_id=1, source_target_pairs={{0,32},{1,33},{2,34},{3,35},{4,36},{5,37},{6,38},{7,39},{8,40},{9,... | collective-permute-start | bytes 12296 | tf_op jit(solution)/shard_map/ppermute | solution.py:8
  115.1 39.8 %slice-start = ((s8[6291456]{0:T(1024)(128)(4,1)}), s8[2097152]{0:T(1024)(128)(4,1)S(1)}, s32[]{:S(2)}) async-start(s8[6291456]{0:T(1024)(128)(4,1)} %bitcast.21), calls=%async_computation | async-start | bytes 4194304
  146.8 8.1 %slice-start.1 = ((s8[6291456]{0:T(1024)(128)(4,1)}), s8[4194304]{0:T(1024)(128)(4,1)S(1)}, s32[]{:S(2)}) async-start(s8[6291456]{0:T(1024)(128)(4,1)} %bitcast.21), calls=%async_computation.1 | async-start | bytes 8388608
  149.6 34.3 %collective-permute-start.2 = (bf16[1024,768]{1,0:T(8,128)(2,1)}, bf16[1024,768]{1,0:T(8,128)(2,1)}, u32[]{:S(2)}, u32[]{:S(2)}) collective-permute-start(bf16[1024,768]{1,0:T(8,128)(2,1)} %slice.84), channel_id=1, source_target_pairs={{0,32},{1,33},{2,34},{3,35},{4,36},{5,37},{6,38},{7,39},{8,40},{9,... | collective-permute-start | bytes 4718600 | tf_op jit(solution)/shard_map/ppermute | solution.py:8
where the time goes:
time: 283 us; the launch traced here: 282 us
  blocking collectives  68.5 us (24%)
  other arithmetic  66.6 us (24%)
  local copies, waits for them, and re-layouts  66.4 us (23%)
  waiting for transfers between devices  59.6 us (21%)
  matrix products  12.2 us (4%)
  between operations  4.75 us (2%)
  starting transfers between devices  4.2 us (1%)
    psum x1, blocking collectives, local(): total_one, number_one = lax.psum((part_one, tally_one), 'cube')  68.5 us
    ppermute x4, waiting for transfers between devices, from_partner(): lax.ppermute(shard, axis, [(i, i ^ 1 << stride) for i in range(lax.axis_s...  59.6 us
    scatter x3, local copies, waits for them, and re-layouts, compact(): return base.at[index].set(rows)[:cap]  58.5 us
    scatter x1, other arithmetic, compact(): return base.at[index].set(rows)[:cap]  31.5 us
    dot_general x2, matrix products, split_margin(): jnp.dot(held_rows, pair.astype(jnp.bfloat16).T, preferred_element_type=jn...  12.2 us
    reduce_sum x1, other arithmetic, local(): jnp.sum(held_two, axis=0, dtype=jnp.float32)[None]  11.5 us
    select_n x1, other arithmetic, local(): jnp.where(moving[:, None], jnp.zeros((), jnp.bfloat16), held_one)  7.02 us
  transfers between devices with their start and end apart: 4, of which 3 were waited for; matrix products, arithmetic and copies ran while one was open for 22% of the time, Pallas kernels for 0%

commit v1 on v0

v1 whole, which is shorter than its diff:
```python
import jax
import jax.numpy as jnp
from jax import lax
from jax.experimental import pallas as pl
from jax.experimental.pallas import tpu as pltpu
from jax.sharding import PartitionSpec as P

MESH = pl.DeviceIdType.MESH
ROWS = 4096
WIDTH = 768
CAP_ONE = 2048
CAP_TWO = 1024
HALF = 512
CHUNK = 256
HELD = ROWS + CAP_ONE + CAP_TWO
F32 = jnp.float32
BF16 = jnp.bfloat16

CHUNKS = 12


def split3(v):
    hi = v.astype(BF16).astype(F32)
    mid = (v - hi).astype(BF16).astype(F32)
    lo = v - hi - mid
    return hi, mid, lo


def stack_rows(rows, count):
    at = lax.broadcasted_iota(jnp.int32, (count, rows[0].shape[1]), 0)
    out = jnp.zeros(at.shape, rows[0].dtype)
    for k, row in enumerate(rows):
        out = jnp.where(at == k, row, out)
    return out


def exchange_kernel(
    x_ref, lab_ref,
    held, m1, m2, cent,
    xv, ybuf, dland, lhs, rk, acc, accs, arl, vmat, ms_c, ms_b, ms_d, ml_c, ml_b, ml_d,
    load_sem, ar_send, ar_recv, row_send, row_recv, m_send, m_recv,
):
    me = lax.axis_index("cube")
    xi = me // 32
    yi = (me // 8) % 4
    zi = (me // 2) % 4
    t = me // 64
    u = xi % 2

    def three(i, stride):
        return [
            me + stride * (1 - 2 * (i % 2)),
            me + stride * (2 - 4 * (i // 2)),
            me + stride * (3 - 2 * i),
        ]

    x1, x2, x3 = three(xi, 32)
    phases = [[x1, x2, x3], three(zi, 2), three(yi, 8), [me + 1 - 2 * (me % 2)]]
    partners = [d for phase in phases for d in phase]

    barrier = pltpu.get_barrier_semaphore()
    for d in partners:
        pl.semaphore_signal(barrier, inc=1, device_id=(d,), device_id_type=MESH)

    loads = [
        pltpu.make_async_copy(x_ref.at[pl.ds(i * 1024, 1024)], xv.at[pl.ds(i * 1024, 1024)], load_sem.at[i])
        for i in range(4)
    ]
    for c in loads:
        c.start()

    first = lab_ref[0:1, :]
    later = lab_ref[1:2, :]
    leave = first != t
    move = later != u
    f_leave = jnp.where(leave, 1.0, 0.0)
    f_move = jnp.where(move, 1.0, 0.0)
    f_b = f_move * (1.0 - f_leave)
    f_d = f_move * f_leave
    kinds = stack_rows([f_leave, f_b, f_d], 16).astype(BF16)
    tri = jnp.where(
        lax.broadcasted_iota(jnp.int32, (256, 256), 0) <= lax.broadcasted_iota(jnp.int32, (256, 256), 1), 1.0, 0.0
    ).astype(BF16)
    carry = jnp.full((16, 1), -1.0, F32)
    for k in range(ROWS // 256):
        part = kinds[:, 256 * k : 256 * k + 256]
        run = jnp.dot(part, tri, preferred_element_type=F32) + carry
        carry = run[:, 255:256]
        place = run.astype(jnp.int32)
        s = pl.ds(256 * k, 256)
        lv = leave[:, 256 * k : 256 * k + 256]
        mv = move[:, 256 * k : 256 * k + 256]
        none = jnp.full((1, 256), -1, jnp.int32)
        rk[0:1, s] = jnp.where(mv, none, jnp.where(lv, place[0:1], none))
        rk[1:2, s] = jnp.where(lv, none, jnp.where(mv, place[1:2], none))
        rk[2:3, s] = jnp.where(lv, jnp.where(mv, place[2:3], none), none)
        rk[3:4, s] = jnp.where(lv, place[0:1], none)
    n_b = carry[1:2, 0:1] + 1.0

    def one_hot(row, base):
        for k in range(ROWS // 256):
            s = pl.ds(256 * k, 256)
            at = lax.broadcasted_iota(jnp.int32, (CHUNK, 256), 0)
            want = rk[pl.ds(row, 1), s] - base
            lhs[0:CHUNK, s] = jnp.where(at == want, 1.0, 0.0).astype(BF16)

    one_hot(0, 0)
    group = 2 * first + later
    masks = stack_rows([jnp.where(group == g, 1.0, 0.0) for g in range(4)], 16)
    lhs[CHUNK : CHUNK + 16, :] = masks.astype(BF16)
    count = jnp.sum(masks[0:4], axis=1, keepdims=True)
    for c in loads:
        c.wait()
    out = jnp.dot(lhs[...], xv[...], preferred_element_type=F32)
    ybuf[0:CHUNK, :] = out[0:CHUNK].astype(BF16)
    accs[0, 0:4, :] = out[CHUNK : CHUNK + 4]
    accs[0, 4:8, :] = jnp.broadcast_to(count, (4, WIDTH))
    pl.semaphore_wait(barrier, len(partners))

    def ar_copies(p):
        base = 3 * p
        return [
            pltpu.make_async_remote_copy(
                src_ref=accs.at[p], dst_ref=arl.at[base + i], send_sem=ar_send.at[base + i],
                recv_sem=ar_recv.at[base + i], device_id=(d,), device_id_type=MESH,
            )
            for i, d in enumerate(phases[p])
        ]

    def ar_start(p):
        for c in ar_copies(p):
            c.start()

    def ar_finish(p):
        for c in ar_copies(p):
            c.wait()
        if p < 3:
            total = (accs[p] + arl[3 * p]) + (arl[3 * p + 1] + arl[3 * p + 2])
            accs[p + 1] = total
        else:
            acc[...] = accs[3] + arl[9]

    def c_copy(q):
        j = jnp.where(q == 0, 0, q - 4)
        return pltpu.make_async_remote_copy(
            src_ref=ybuf.at[pl.ds(pl.multiple_of(q * CHUNK, CHUNK), CHUNK)],
            dst_ref=held.at[pl.ds(pl.multiple_of(ROWS + j * CHUNK, CHUNK), CHUNK)],
            send_sem=row_send.at[q], recv_sem=row_recv.at[q], device_id=(x2,), device_id_type=MESH,
        )

    def b_copy(q):
        return pltpu.make_async_remote_copy(
            src_ref=ybuf.at[pl.ds(pl.multiple_of(q * CHUNK, CHUNK), CHUNK)],
            dst_ref=held.at[pl.ds(pl.multiple_of(ROWS + CAP_ONE + (q - 1) * CHUNK, CHUNK), CHUNK)],
            send_sem=row_send.at[q], recv_sem=row_recv.at[q], device_id=(x1,), device_id_type=MESH,
        )

    def d_copy(q):
        return pltpu.make_async_remote_copy(
            src_ref=ybuf.at[pl.ds(pl.multiple_of(q * CHUNK, CHUNK), CHUNK)],
            dst_ref=dland.at[pl.ds(pl.multiple_of((q - 3) * CHUNK, CHUNK), CHUNK)],
            send_sem=row_send.at[q], recv_sem=row_recv.at[q], device_id=(x3,), device_id_type=MESH,
        )

    ar_start(0)
    c_copy(0).start()

    def compact(q, row, base):
        one_hot(row, base)
        res = jnp.dot(lhs[0:CHUNK, :], xv[...], preferred_element_type=F32)
        ybuf[pl.ds(pl.multiple_of(q * CHUNK, CHUNK), CHUNK), :] = res.astype(BF16)

    def early(q, _):
        row = jnp.where(q < 3, 1, jnp.where(q < 5, 2, 0))
        base = CHUNK * jnp.where(q < 3, q - 1, jnp.where(q < 5, q - 3, q - 4))
        compact(q, row, base)

        @pl.when(q < 3)
        def _():
            b_copy(q).start()

        @pl.when((q >= 3) & (q < 5))
        def _():
            d_copy(q).start()

        @pl.when(q >= 5)
        def _():
            c_copy(q).start()

        for p in range(4):
            @pl.when(q == p + 1)
            def _(p=p):
                ar_finish(p)
                if p < 3:
                    ar_start(p + 1)

        return 0

    lax.fori_loop(1, 9, early, 0)

    tot = acc[...]
    c2 = tot[0:4] / tot[4:8]
    pair_sum = jnp.concatenate([tot[0:1] + tot[1:2], tot[2:3] + tot[3:4]], axis=0)
    pair_num = jnp.concatenate([tot[4:5] + tot[5:6], tot[6:7] + tot[7:8]], axis=0)
    c1 = pair_sum / pair_num
    cent[0:2, :] = c1
    cent[2:6, :] = c2
    six = jnp.concatenate([c1, c2, jnp.zeros((2, WIDTH), F32)], axis=0)
    norm = jnp.sum(six * six, axis=1, keepdims=True)
    off_one = 0.5 * (norm[1:2] - norm[0:1])
    off_low = 0.5 * (norm[3:4] - norm[2:3])
    off_high = 0.5 * (norm[5:6] - norm[4:5])
    sixb = jnp.concatenate([six, jnp.zeros((8, WIDTH), F32)], axis=0).astype(BF16)

    def margins(k, _):
        s = pl.ds(pl.multiple_of(k * 512, 512), 512)
        sc = lax.dot_general(sixb, xv[s, :], (((1,), (1,)), ((), ())), preferred_element_type=F32)
        fk = lab_ref[0:1, s]
        mk = lab_ref[1:2, s] != u
        lk = fk != t
        one = (sc[1:2] - sc[0:1] - off_one) / WIDTH
        two = jnp.where(fk == 1, sc[5:6] - sc[4:5] - off_high, sc[3:4] - sc[2:3] - off_low) / WIDTH
        m1[0:1, s] = jnp.where(lk, 0.0, one)
        m2[0:1, s] = jnp.where(lk, 0.0, jnp.where(mk, 0.0, two))
        two_c = jnp.where(mk, 0.0, two)
        vmat[:, s] = stack_rows([*split3(one), *split3(two_c), *split3(two)], 16).astype(BF16)
        return 0

    lax.fori_loop(0, 8, margins, 0)

    def pack_margins(row, base):
        one_hot(row, base)
        return lax.dot_general(
            vmat[...], lhs[0:CHUNK, :], (((1,), (1,)), ((), ())), preferred_element_type=F32
        )

    def pack_c(j, _):
        r = pack_margins(3, CHUNK * j)
        s = pl.ds(pl.multiple_of(j * CHUNK, CHUNK), CHUNK)
        ms_c[0:1, s] = r[0:1] + r[1:2] + r[2:3]
        ms_c[1:2, s] = r[3:4] + r[4:5] + r[5:6]
        return 0

    def pack_bd(j, _):
        r = pack_margins(1 + j // 2, CHUNK * (j % 2))
        s = pl.ds(pl.multiple_of((j % 2) * CHUNK, CHUNK), CHUNK)
        v = r[6:7] + r[7:8] + r[8:9]

        @pl.when(j < 2)
        def _():
            ms_b[0:1, s] = v

        @pl.when(j >= 2)
        def _():
            ms_d[0:1, s] = v

        return 0

    ms_b[1:2, :] = jnp.broadcast_to(n_b, (1, HALF))
    ms_d[1:2, :] = jnp.zeros((1, HALF), F32)
    lax.fori_loop(0, 4, pack_bd, 0)
    m_copies = [
        pltpu.make_async_remote_copy(
            src_ref=src, dst_ref=dst, send_sem=m_send.at[i], recv_sem=m_recv.at[i], device_id=(d,), device_id_type=MESH,
        )
        for i, (src, dst, d) in enumerate([(ms_b, ml_b, x1), (ms_d, ml_d, x3), (ms_c, ml_c, x2)])
    ]
    m_copies[0].start()
    m_copies[1].start()
    lax.fori_loop(0, 8, pack_c, 0)
    m_copies[2].start()

    def late(q, _):
        compact(q, 0, CHUNK * (q - 4))
        c_copy(q).start()
        return 0

    lax.fori_loop(9, CHUNKS, late, 0)

    def keep(k, _):
        s = pl.ds(pl.multiple_of(k * 256, 256), 256)
        stay = jnp.where(lab_ref[0:1, s] == t, jnp.where(lab_ref[1:2, s] == u, 1.0, 0.0), 0.0)
        eye = lax.broadcasted_iota(jnp.int32, (256, 256), 0) == lax.broadcasted_iota(jnp.int32, (256, 256), 1)
        pick = jnp.where(eye, stay, 0.0).astype(BF16)
        held[s, :] = jnp.dot(pick, xv[s, :], preferred_element_type=F32).astype(BF16)
        return 0

    lax.fori_loop(0, ROWS // 256, keep, 0)

    for c in m_copies[:2]:
        c.wait()
    for q in (1, 2):
        b_copy(q).wait()
    for q in (3, 4):
        d_copy(q).wait()
    shift = ml_b[1:2, 0:1].astype(jnp.int32)

    def place(k, _):
        base = k * 256
        s = pl.ds(pl.multiple_of(ROWS + CAP_ONE + base, 256), 256)
        slot = lax.broadcasted_iota(jnp.int32, (256, HALF), 0) + base
        src = lax.broadcasted_iota(jnp.int32, (256, HALF), 1) + shift
        hot = jnp.where(slot == src, 1.0, 0.0).astype(BF16)
        rows = jnp.dot(hot, dland[...], preferred_element_type=F32)

        @pl.when(k < 2)
        def _():
            held[s, :] = (rows + held[s, :].astype(F32)).astype(BF16)

        @pl.when(k >= 2)
        def _():
            held[s, :] = rows.astype(BF16)

        return 0

    lax.fori_loop(0, 4, place, 0)
    dm = stack_rows(list(split3(ml_d[0:1, :])), 16).astype(BF16)
    src = lax.broadcasted_iota(jnp.int32, (HALF, CAP_TWO), 0) + shift
    slot = lax.broadcasted_iota(jnp.int32, (HALF, CAP_TWO), 1)
    moved = jnp.dot(dm, jnp.where(slot == src, 1.0, 0.0).astype(BF16), preferred_element_type=F32)
    moved = moved[0:1] + moved[1:2] + moved[2:3]
    m2[0:1, ROWS + CAP_ONE : ROWS + CAP_ONE + HALF] = moved[:, 0:HALF] + ml_b[0:1, :]
    m2[0:1, ROWS + CAP_ONE + HALF : HELD] = moved[:, HALF:CAP_TWO]
    m_copies[2].wait()
    m1[0:1, ROWS : ROWS + CAP_ONE] = ml_c[0:1, :]
    m2[0:1, ROWS : ROWS + CAP_ONE] = ml_c[1:2, :]

    for q in (0, 5, 6, 7, 8, 9, 10, 11):
        c_copy(q).wait()


PIECES = 14


def store_kernel(held, m1, m2, cent, held_out, m1_out, m2_out, cent_out, sem):
    step = HELD // PIECES
    copies = [
        pltpu.make_async_copy(held.at[pl.ds(i * step, step)], held_out.at[pl.ds(i * step, step)], sem.at[i])
        for i in range(PIECES)
    ]
    for i, (src, dst) in enumerate([(m1, m1_out), (m2, m2_out), (cent, cent_out)]):
        copies.append(pltpu.make_async_copy(src, dst, sem.at[PIECES + i]))
    for c in copies:
        c.start()
    for c in copies:
        c.wait()


def local(vectors, child_labels):
    in_vmem = pl.BlockSpec(memory_space=pltpu.VMEM)
    anywhere = pl.BlockSpec(memory_space=pl.ANY)
    shapes = [((HELD, WIDTH), BF16), ((1, ROWS + CAP_ONE), F32), ((1, HELD), F32), ((6, WIDTH), F32)]
    dma = pltpu.SemaphoreType.DMA
    parts = pl.pallas_call(
        exchange_kernel,
        out_shape=tuple(pltpu.VMEM(s, d) for s, d in shapes),
        in_specs=[anywhere, in_vmem],
        out_specs=(in_vmem,) * 4,
        scratch_shapes=[
            pltpu.VMEM((ROWS, WIDTH), BF16),
            pltpu.VMEM((CHUNKS * CHUNK, WIDTH), BF16),
            pltpu.VMEM((HALF, WIDTH), BF16),
            pltpu.VMEM((CHUNK + 16, ROWS), BF16),
            pltpu.VMEM((8, ROWS), jnp.int32),
            pltpu.VMEM((8, WIDTH), F32),
            pltpu.VMEM((4, 8, WIDTH), F32),
            pltpu.VMEM((10, 8, WIDTH), F32),
            pltpu.VMEM((16, ROWS), BF16),
            pltpu.VMEM((2, CAP_ONE), F32),
            pltpu.VMEM((2, HALF), F32),
            pltpu.VMEM((2, HALF), F32),
            pltpu.VMEM((2, CAP_ONE), F32),
            pltpu.VMEM((2, HALF), F32),
            pltpu.VMEM((2, HALF), F32),
            dma((4,)),
            dma((10,)),
            dma((10,)),
            dma((CHUNKS,)),
            dma((CHUNKS,)),
            dma((3,)),
            dma((3,)),
        ],
        compiler_params=pltpu.CompilerParams(
            collective_id=0, has_side_effects=True, vmem_limit_bytes=44 << 20
        ),
        name="exchange",
    )(vectors, child_labels)
    held, m1, m2, cent = pl.pallas_call(
        store_kernel,
        out_shape=tuple(jax.ShapeDtypeStruct(s, d) for s, d in shapes),
        in_specs=[in_vmem] * 4,
        out_specs=(anywhere,) * 4,
        scratch_shapes=[dma((PIECES + 3,))],
        compiler_params=pltpu.CompilerParams(vmem_limit_bytes=16 << 20),
        name="store",
    )(*parts)
    return held, m1.reshape(-1), m2.reshape(-1), cent


def solution(mesh):
    return jax.shard_map(
        local,
        mesh=mesh,
        in_specs=(P("cube", None), P(None, "cube")),
        out_specs=(P("cube", None), P("cube"), P("cube"), P()),
        check_vma=False,
    )
```

time: 283 us -> 105 us (0.37)
  Pallas kernels: 0 us -> 103 us
  blocking collectives: 68.5 us -> 0 us
  other arithmetic: 66.6 us -> 0 us
  local copies, waits for them, and re-layouts: 66.4 us -> 0 us
  waiting for transfers between devices: 59.6 us -> 0 us
  matrix products: 12.2 us -> 0 us
  starting transfers between devices: 4.2 us -> 0 us
  between operations: 4.75 us -> 0.64 us
    pallas_call x0 -> x2, Pallas kernels: none -> 103 us  [the longest x1 98.9 us: local(): pl.pallas_call(exchange_kernel, out_shape=tuple((pltpu.VMEM(s, d) for s,...]
    psum x1 -> x0, blocking collectives: 68.5 us -> none  [local(): total_one, number_one = lax.psum((part_one, tally_one), 'cube')]
    ppermute x4 -> x0, waiting for transfers between devices: 59.6 us -> none  [from_partner(): lax.ppermute(shard, axis, [(i, i ^ 1 << stride) for i in range(lax.axis_s...]
    scatter x3 -> x0, local copies, waits for them, and re-layouts: 58.5 us -> none  [compact(): return base.at[index].set(rows)[:cap]]
    scatter x1 -> x0, other arithmetic: 31.5 us -> none  [compact(): return base.at[index].set(rows)[:cap]]
    reduce_sum x6 -> x0, other arithmetic: 19.2 us -> none  [the longest x1 11.5 us: local(): jnp.sum(held_two, axis=0, dtype=jnp.float32)[None]]
    select_n x7 -> x0, other arithmetic: 13.2 us -> none  [the longest x1 7.02 us: local(): jnp.where(moving[:, None], jnp.zeros((), jnp.bfloat16), held_one)]
    dot_general x2 -> x0, matrix products: 12.2 us -> none  [split_margin(): jnp.dot(held_rows, pair.astype(jnp.bfloat16).T, preferred_element_type=jn...]
  transfers between devices with their start and end apart: 4 -> 0, of which waited for: 3 -> 0; matrix products, arithmetic and copies ran while one was open for 22% -> 0% of each run, Pallas kernels for 0% -> 0%
where the time goes in v1:
time: 105 us; the launch traced here: 104 us
  Pallas kernels  103 us (98%)
    pallas_call x1, Pallas kernels, local(): pl.pallas_call(exchange_kernel, out_shape=tuple((pltpu.VMEM(s, d) for s,...  98.9 us
    pallas_call x1, Pallas kernels, local(): pl.pallas_call(store_kernel, out_shape=tuple((jax.ShapeDtypeStruct(s, d)...  4.25 us

profile of v1, /device:TPU:1, one launch (start us, length us, event | category | flops | bytes accessed | tf_op | source)
XLA Modules:
  0.0 103.8 jit_solution(10437582581077832345)
XLA Ops:
  0.6 98.9 %exchange.1 = (bf16[7168,768]{1,0:T(8,128)(2,1)S(1)}, f32[1,6144]{1,0:T(1,128)S(1)}, f32[1,7168]{1,0:T(1,128)S(1)}, f32[6,768]{1,0:T(8,128)S(1)}) custom-call(bf16[4096,768]{1,0:T(8,128)(2,1)} %x_ref.1, s32[2,4096]{1,0:T(2,128)} %lab_ref.1), custom_call_target="tpu_custom_call" | custom-call | tf_op jit(solution)/shard_map/exchange/pallas_call | solution.py:354
  99.5 4.2 %store.1 = (bf16[7168,768]{1,0:T(8,128)(2,1)}, f32[1,6144]{1,0:T(1,128)}, f32[1,7168]{1,0:T(1,128)}, f32[6,768]{1,0:T(8,128)}) custom-call(bf16[7168,768]{1,0:T(8,128)(2,1)S(1)} %get-tuple-element.12.held, f32[1,6144]{1,0:T(1,128)S(1)} %get-tuple-element.13.m1, f32[1,7168]{1,0:T(1,128)S(1)} %get-tuple-element.14.m2, f32[6,768]{1,0:T(8,128)S(1)} %get-tuple-element.15.cent), custom_call_target="tpu_custom_call" | custom-call | tf_op jit(solution)/shard_map/store/pallas_call | solution.py:388

commit v2 on v1

--- a/solution.py
+++ b/solution.py
@@ -11,12 +11,21 @@
 CAP_ONE = 2048
 CAP_TWO = 1024
 HALF = 512
+LOAD = 1024
+AHEAD = 2
+PIECE = 512
 CHUNK = 256
 HELD = ROWS + CAP_ONE + CAP_TWO
 F32 = jnp.float32
 BF16 = jnp.bfloat16
 
-CHUNKS = 12
+HEAD = 128
+MID = 4
+C_CHUNKS = 8
+B_AT = HEAD + C_CHUNKS * CHUNK
+D_AT = B_AT + HALF
+PACKED = D_AT + HALF
+SUM_ROWS = 16
 
 
 def split3(v):
@@ -35,12 +44,20 @@
 
 
 def exchange_kernel(
-    x_ref, lab_ref,
+    x_ref, lab_any,
     held, m1, m2, cent,
-    xv, ybuf, dland, lhs, rk, acc, accs, arl, vmat, ms_c, ms_b, ms_d, ml_c, ml_b, ml_d,
+    xv, lab_ref, ybuf, dland, lhs, rk, acc, accs, arl, vmat, ms_c, ms_b, ms_d, ml_c, ml_b, ml_d,
     load_sem, ar_send, ar_recv, row_send, row_recv, m_send, m_recv,
 ):
     me = lax.axis_index("cube")
+    loads = [
+        pltpu.make_async_copy(x_ref.at[pl.ds(i * LOAD, LOAD)], xv.at[pl.ds(i * LOAD, LOAD)], load_sem.at[i])
+        for i in range(ROWS // LOAD)
+    ]
+    lab_load = pltpu.make_async_copy(lab_any, lab_ref, load_sem.at[ROWS // LOAD])
+    lab_load.start()
+    for c in loads[:AHEAD]:
+        c.start()
     xi = me // 32
     yi = (me // 8) % 4
     zi = (me // 2) % 4
@@ -55,19 +72,17 @@
         ]
 
     x1, x2, x3 = three(xi, 32)
-    phases = [[x1, x2, x3], three(zi, 2), three(yi, 8), [me + 1 - 2 * (me % 2)]]
+    z1, z2, _ = three(zi, 2)
+    y1, y2, _ = three(yi, 8)
+    phases = [[x1, x2, x3], [z1], [z2], [y1], [y2], [me + 1 - 2 * (me % 2)]]
+    slots = [0, 3, 4, 5, 6, 7]
     partners = [d for phase in phases for d in phase]
 
     barrier = pltpu.get_barrier_semaphore()
     for d in partners:
         pl.semaphore_signal(barrier, inc=1, device_id=(d,), device_id_type=MESH)
 
-    loads = [
-        pltpu.make_async_copy(x_ref.at[pl.ds(i * 1024, 1024)], xv.at[pl.ds(i * 1024, 1024)], load_sem.at[i])
-        for i in range(4)
-    ]
-    for c in loads:
-        c.start()
+    lab_load.wait()
 
     first = lab_ref[0:1, :]
     later = lab_ref[1:2, :]
@@ -77,15 +92,15 @@
     f_move = jnp.where(move, 1.0, 0.0)
     f_b = f_move * (1.0 - f_leave)
     f_d = f_move * f_leave
-    kinds = stack_rows([f_leave, f_b, f_d], 16).astype(BF16)
+    kinds = stack_rows([f_leave, f_b, f_d], 16)
     tri = jnp.where(
         lax.broadcasted_iota(jnp.int32, (256, 256), 0) <= lax.broadcasted_iota(jnp.int32, (256, 256), 1), 1.0, 0.0
     ).astype(BF16)
     carry = jnp.full((16, 1), -1.0, F32)
     for k in range(ROWS // 256):
         part = kinds[:, 256 * k : 256 * k + 256]
-        run = jnp.dot(part, tri, preferred_element_type=F32) + carry
-        carry = run[:, 255:256]
+        run = jnp.dot(part.astype(BF16), tri, preferred_element_type=F32) + carry
+        carry = carry + jnp.sum(part, axis=1, keepdims=True)
         place = run.astype(jnp.int32)
         s = pl.ds(256 * k, 256)
         lv = leave[:, 256 * k : 256 * k + 256]
@@ -104,21 +119,24 @@
             want = rk[pl.ds(row, 1), s] - base
             lhs[0:CHUNK, s] = jnp.where(at == want, 1.0, 0.0).astype(BF16)
 
-    one_hot(0, 0)
-    group = 2 * first + later
-    masks = stack_rows([jnp.where(group == g, 1.0, 0.0) for g in range(4)], 16)
-    lhs[CHUNK : CHUNK + 16, :] = masks.astype(BF16)
-    count = jnp.sum(masks[0:4], axis=1, keepdims=True)
-    for c in loads:
+    def hot_piece(row, base, count, at, size):
+        slot = lax.broadcasted_iota(jnp.int32, (count, size), 0)
+        return jnp.where(slot == rk[pl.ds(row, 1), pl.ds(at, size)] - base, 1.0, 0.0).astype(BF16)
+
+    out = jnp.zeros((HEAD, WIDTH), F32)
+    for i, c in enumerate(loads):
         c.wait()
-    out = jnp.dot(lhs[...], xv[...], preferred_element_type=F32)
-    ybuf[0:CHUNK, :] = out[0:CHUNK].astype(BF16)
-    accs[0, 0:4, :] = out[CHUNK : CHUNK + 4]
-    accs[0, 4:8, :] = jnp.broadcast_to(count, (4, WIDTH))
+        if i + AHEAD < len(loads):
+            loads[i + AHEAD].start()
+        hot = hot_piece(0, 0, HEAD, i * LOAD, LOAD)
+        out = out + jnp.dot(hot, xv[pl.ds(i * LOAD, LOAD), :], preferred_element_type=F32)
+    ybuf[0:HEAD, :] = out.astype(BF16)
     pl.semaphore_wait(barrier, len(partners))
 
+    LAST = len(phases) - 1
+
     def ar_copies(p):
-        base = 3 * p
+        base = slots[p]
         return [
             pltpu.make_async_remote_copy(
                 src_ref=accs.at[p], dst_ref=arl.at[base + i], send_sem=ar_send.at[base + i],
@@ -134,74 +152,98 @@
     def ar_finish(p):
         for c in ar_copies(p):
             c.wait()
-        if p < 3:
-            total = (accs[p] + arl[3 * p]) + (arl[3 * p + 1] + arl[3 * p + 2])
+        base = slots[p]
+        total = accs[p] + arl[base]
+        if len(phases[p]) == 3:
+            total = total + (arl[base + 1] + arl[base + 2])
+        if p < LAST:
             accs[p + 1] = total
         else:
-            acc[...] = accs[3] + arl[9]
-
-    def c_copy(q):
-        j = jnp.where(q == 0, 0, q - 4)
+            acc[...] = total
+
+    def rows_copy(k, src, dst, start, count, to):
         return pltpu.make_async_remote_copy(
-            src_ref=ybuf.at[pl.ds(pl.multiple_of(q * CHUNK, CHUNK), CHUNK)],
-            dst_ref=held.at[pl.ds(pl.multiple_of(ROWS + j * CHUNK, CHUNK), CHUNK)],
-            send_sem=row_send.at[q], recv_sem=row_recv.at[q], device_id=(x2,), device_id_type=MESH,
+            src_ref=ybuf.at[pl.ds(pl.multiple_of(src, HEAD), count)],
+            dst_ref=dst.at[pl.ds(pl.multiple_of(start, HEAD), count)],
+            send_sem=row_send.at[k], recv_sem=row_recv.at[k], device_id=(to,), device_id_type=MESH,
         )
 
-    def b_copy(q):
-        return pltpu.make_async_remote_copy(
-            src_ref=ybuf.at[pl.ds(pl.multiple_of(q * CHUNK, CHUNK), CHUNK)],
-            dst_ref=held.at[pl.ds(pl.multiple_of(ROWS + CAP_ONE + (q - 1) * CHUNK, CHUNK), CHUNK)],
-            send_sem=row_send.at[q], recv_sem=row_recv.at[q], device_id=(x1,), device_id_type=MESH,
-        )
-
-    def d_copy(q):
-        return pltpu.make_async_remote_copy(
-            src_ref=ybuf.at[pl.ds(pl.multiple_of(q * CHUNK, CHUNK), CHUNK)],
-            dst_ref=dland.at[pl.ds(pl.multiple_of((q - 3) * CHUNK, CHUNK), CHUNK)],
-            send_sem=row_send.at[q], recv_sem=row_recv.at[q], device_id=(x3,), device_id_type=MESH,
-        )
-
+    def c_copy(j, count=CHUNK):
+        src = HEAD + j * CHUNK
+        return rows_copy(4 + j, src, held, ROWS + src, count, x2)
+
+    def b_copy(j):
+        return rows_copy(2 * j, B_AT + j * CHUNK, held, ROWS + CAP_ONE + j * CHUNK, CHUNK, x1)
+
+    def d_copy(j):
+        return rows_copy(2 * j + 1, D_AT + j * CHUNK, dland, j * CHUNK, CHUNK, x3)
+
+    head_copy = rows_copy(4 + C_CHUNKS, 0, held, ROWS, HEAD, x2)
+    last_copy = c_copy(MID, CAP_ONE - HEAD - MID * CHUNK)
+    head_copy.start()
+
+    def compact(row, base, to):
+        res = jnp.zeros((CHUNK, WIDTH), F32)
+        for k in range(ROWS // PIECE):
+            hot = hot_piece(row, base, CHUNK, k * PIECE, PIECE)
+            res = res + jnp.dot(hot, xv[pl.ds(k * PIECE, PIECE), :], preferred_element_type=F32)
+        ybuf[pl.ds(pl.multiple_of(to, HEAD), CHUNK), :] = res.astype(BF16)
+
+    group = 2 * first + later
+    masks = stack_rows([jnp.where(group == g, 1.0, 0.0) for g in range(4)], SUM_ROWS)
+    count = jnp.sum(masks[0:4], axis=1, keepdims=True)
+    res = jnp.zeros((CHUNK + SUM_ROWS, WIDTH), F32)
+    for k in range(ROWS // PIECE):
+        hot = hot_piece(0, HEAD, CHUNK, k * PIECE, PIECE)
+        both = jnp.concatenate([hot, masks[:, k * PIECE : (k + 1) * PIECE].astype(BF16)], axis=0)
+        res = res + jnp.dot(both, xv[pl.ds(k * PIECE, PIECE), :], preferred_element_type=F32)
+    ybuf[HEAD : HEAD + CHUNK, :] = res[0:CHUNK].astype(BF16)
+    accs[0, :, 0:WIDTH] = res[CHUNK : CHUNK + 4]
+    accs[0, :, WIDTH:] = jnp.broadcast_to(count, (4, 128))
     ar_start(0)
     c_copy(0).start()
 
-    def compact(q, row, base):
-        one_hot(row, base)
-        res = jnp.dot(lhs[0:CHUNK, :], xv[...], preferred_element_type=F32)
-        ybuf[pl.ds(pl.multiple_of(q * CHUNK, CHUNK), CHUNK), :] = res.astype(BF16)
-
-    def early(q, _):
-        row = jnp.where(q < 3, 1, jnp.where(q < 5, 2, 0))
-        base = CHUNK * jnp.where(q < 3, q - 1, jnp.where(q < 5, q - 3, q - 4))
-        compact(q, row, base)
-
-        @pl.when(q < 3)
+    def ar_step(p):
+        ar_finish(p)
+        if p < LAST:
+            ar_start(p + 1)
+
+    def early_bd(k, _):
+        j = k // 2
+        compact(1 + k % 2, CHUNK * j, B_AT + HALF * (k % 2) + CHUNK * j)
+
+        @pl.when(k % 2 == 1)
         def _():
-            b_copy(q).start()
-
-        @pl.when((q >= 3) & (q < 5))
-        def _():
-            d_copy(q).start()
-
-        @pl.when(q >= 5)
-        def _():
-            c_copy(q).start()
+            b_copy(j).start()
+            d_copy(j).start()
 
         for p in range(4):
-            @pl.when(q == p + 1)
+            @pl.when(k == p)
             def _(p=p):
-                ar_finish(p)
-                if p < 3:
-                    ar_start(p + 1)
-
-        return 0
-
-    lax.fori_loop(1, 9, early, 0)
-
-    tot = acc[...]
-    c2 = tot[0:4] / tot[4:8]
+                ar_step(p)
+
+        return 0
+
+    lax.fori_loop(0, 4, early_bd, 0)
+
+    def early_c(j, _):
+        compact(0, HEAD + CHUNK * j, HEAD + CHUNK * j)
+        c_copy(j).start()
+
+        for p in range(4, len(phases)):
+            @pl.when(j == p - 3)
+            def _(p=p):
+                ar_step(p)
+
+        return 0
+
+    lax.fori_loop(1, MID, early_c, 0)
+
+    tot = acc[:, 0:WIDTH]
+    num = acc[:, WIDTH : WIDTH + 1]
+    c2 = tot / num
     pair_sum = jnp.concatenate([tot[0:1] + tot[1:2], tot[2:3] + tot[3:4]], axis=0)
-    pair_num = jnp.concatenate([tot[4:5] + tot[5:6], tot[6:7] + tot[7:8]], axis=0)
+    pair_num = jnp.concatenate([num[0:1] + num[1:2], num[2:3] + num[3:4]], axis=0)
     c1 = pair_sum / pair_num
     cent[0:2, :] = c1
     cent[2:6, :] = c2
@@ -270,12 +312,12 @@
     lax.fori_loop(0, 8, pack_c, 0)
     m_copies[2].start()
 
-    def late(q, _):
-        compact(q, 0, CHUNK * (q - 4))
-        c_copy(q).start()
-        return 0
-
-    lax.fori_loop(9, CHUNKS, late, 0)
+    def late(j, _):
+        compact(0, HEAD + CHUNK * j, HEAD + CHUNK * j)
+        return 0
+
+    lax.fori_loop(MID, C_CHUNKS, late, 0)
+    last_copy.start()
 
     def keep(k, _):
         s = pl.ds(pl.multiple_of(k * 256, 256), 256)
@@ -289,10 +331,9 @@
 
     for c in m_copies[:2]:
         c.wait()
-    for q in (1, 2):
-        b_copy(q).wait()
-    for q in (3, 4):
-        d_copy(q).wait()
+    for j in range(2):
+        b_copy(j).wait()
+        d_copy(j).wait()
     shift = ml_b[1:2, 0:1].astype(jnp.int32)
 
     def place(k, _):
@@ -325,8 +366,10 @@
     m1[0:1, ROWS : ROWS + CAP_ONE] = ml_c[0:1, :]
     m2[0:1, ROWS : ROWS + CAP_ONE] = ml_c[1:2, :]
 
-    for q in (0, 5, 6, 7, 8, 9, 10, 11):
-        c_copy(q).wait()
+    head_copy.wait()
+    for j in range(MID):
+        c_copy(j).wait()
+    last_copy.wait()
 
 
 PIECES = 14
@@ -354,17 +397,18 @@
     parts = pl.pallas_call(
         exchange_kernel,
         out_shape=tuple(pltpu.VMEM(s, d) for s, d in shapes),
-        in_specs=[anywhere, in_vmem],
+        in_specs=[anywhere, anywhere],
         out_specs=(in_vmem,) * 4,
         scratch_shapes=[
             pltpu.VMEM((ROWS, WIDTH), BF16),
-            pltpu.VMEM((CHUNKS * CHUNK, WIDTH), BF16),
+            pltpu.VMEM((2, ROWS), jnp.int32),
+            pltpu.VMEM((PACKED, WIDTH), BF16),
             pltpu.VMEM((HALF, WIDTH), BF16),
-            pltpu.VMEM((CHUNK + 16, ROWS), BF16),
+            pltpu.VMEM((CHUNK, ROWS), BF16),
             pltpu.VMEM((8, ROWS), jnp.int32),
-            pltpu.VMEM((8, WIDTH), F32),
-            pltpu.VMEM((4, 8, WIDTH), F32),
-            pltpu.VMEM((10, 8, WIDTH), F32),
+            pltpu.VMEM((4, WIDTH + 128), F32),
+            pltpu.VMEM((6, 4, WIDTH + 128), F32),
+            pltpu.VMEM((8, 4, WIDTH + 128), F32),
             pltpu.VMEM((16, ROWS), BF16),
             pltpu.VMEM((2, CAP_ONE), F32),
             pltpu.VMEM((2, HALF), F32),
@@ -372,11 +416,11 @@
             pltpu.VMEM((2, CAP_ONE), F32),
             pltpu.VMEM((2, HALF), F32),
             pltpu.VMEM((2, HALF), F32),
-            dma((4,)),
-            dma((10,)),
-            dma((10,)),
-            dma((CHUNKS,)),
-            dma((CHUNKS,)),
+            dma((ROWS // LOAD + 1,)),
+            dma((8,)),
+            dma((8,)),
+            dma((C_CHUNKS + 5,)),
+            dma((C_CHUNKS + 5,)),
             dma((3,)),
             dma((3,)),
         ],

time: 105 us -> 98.6 us (0.939); the launches traced: 104 us -> 98.5 us
  Pallas kernels: 103 us -> 97.8 us
    pallas_call x1, Pallas kernels: 98.9 us -> 93.6 us  [local(): pl.pallas_call(exchange_kernel, out_shape=tuple((pltpu.VMEM(s, d) for s,...]
where the time goes in v2:
time: 98.6 us; the launch traced here: 98.5 us
  Pallas kernels  97.8 us (99%)
    pallas_call x1, Pallas kernels, local(): pl.pallas_call(exchange_kernel, out_shape=tuple((pltpu.VMEM(s, d) for s,...  93.6 us
    pallas_call x1, Pallas kernels, local(): pl.pallas_call(store_kernel, out_shape=tuple((jax.ShapeDtypeStruct(s, d)...  4.25 us

profile of v2, /device:TPU:1, one launch (start us, length us, event | category | flops | bytes accessed | tf_op | source)
XLA Modules:
  0.0 98.5 jit_solution(1675469351463744036)
XLA Ops:
  0.6 93.6 %exchange.1 = (bf16[7168,768]{1,0:T(8,128)(2,1)S(1)}, f32[1,6144]{1,0:T(1,128)S(1)}, f32[1,7168]{1,0:T(1,128)S(1)}, f32[6,768]{1,0:T(8,128)S(1)}) custom-call(bf16[4096,768]{1,0:T(8,128)(2,1)} %x_ref.1, s32[2,4096]{1,0:T(2,128)} %lab_any.1), custom_call_target="tpu_custom_call" | custom-call | tf_op jit(solution)/shard_map/exchange/pallas_call | solution.py:397
  94.2 4.2 %store.1 = (bf16[7168,768]{1,0:T(8,128)(2,1)}, f32[1,6144]{1,0:T(1,128)}, f32[1,7168]{1,0:T(1,128)}, f32[6,768]{1,0:T(8,128)}) custom-call(bf16[7168,768]{1,0:T(8,128)(2,1)S(1)} %get-tuple-element.12.held, f32[1,6144]{1,0:T(1,128)S(1)} %get-tuple-element.13.m1, f32[1,7168]{1,0:T(1,128)S(1)} %get-tuple-element.14.m2, f32[6,768]{1,0:T(8,128)S(1)} %get-tuple-element.15.cent), custom_call_target="tpu_custom_call" | custom-call | tf_op jit(solution)/shard_map/store/pallas_call | solution.py:432

commit v3 on v2

--- a/solution.py
+++ b/solution.py
@@ -12,13 +12,15 @@
 CAP_TWO = 1024
 HALF = 512
 LOAD = 1024
-AHEAD = 2
+AHEAD = 4
 PIECE = 512
 CHUNK = 256
 HELD = ROWS + CAP_ONE + CAP_TWO
 F32 = jnp.float32
 BF16 = jnp.bfloat16
 
+MOST = 1792
+SPLIT = 1536
 HEAD = 128
 MID = 4
 C_CHUNKS = 8
@@ -26,6 +28,7 @@
 D_AT = B_AT + HALF
 PACKED = D_AT + HALF
 SUM_ROWS = 16
+LATE = HEAD + MID * CHUNK
 
 
 def split3(v):
@@ -45,8 +48,8 @@
 
 def exchange_kernel(
     x_ref, lab_any,
-    held, m1, m2, cent,
-    xv, lab_ref, ybuf, dland, lhs, rk, acc, accs, arl, vmat, ms_c, ms_b, ms_d, ml_c, ml_b, ml_d,
+    held, m1, m2, cent, flag, rest, slots_hbm,
+    xv, lab_ref, ybuf, cland, dland, lhs, rk, acc, accs, arl, vmat, ms_c, ms_b, ms_d, ms_s, slots_out, ml_c, ml_b, ml_d,
     load_sem, ar_send, ar_recv, row_send, row_recv, m_send, m_recv,
 ):
     me = lax.axis_index("cube")
@@ -92,7 +95,8 @@
     f_move = jnp.where(move, 1.0, 0.0)
     f_b = f_move * (1.0 - f_leave)
     f_d = f_move * f_leave
-    kinds = stack_rows([f_leave, f_b, f_d], 16)
+    f_c = f_leave * (1.0 - f_move)
+    kinds = stack_rows([f_leave, f_b, f_d, f_c], 16)
     tri = jnp.where(
         lax.broadcasted_iota(jnp.int32, (256, 256), 0) <= lax.broadcasted_iota(jnp.int32, (256, 256), 1), 1.0, 0.0
     ).astype(BF16)
@@ -106,11 +110,12 @@
         lv = leave[:, 256 * k : 256 * k + 256]
         mv = move[:, 256 * k : 256 * k + 256]
         none = jnp.full((1, 256), -1, jnp.int32)
-        rk[0:1, s] = jnp.where(mv, none, jnp.where(lv, place[0:1], none))
+        rk[0:1, s] = jnp.where(mv, none, jnp.where(lv, place[3:4], none))
         rk[1:2, s] = jnp.where(lv, none, jnp.where(mv, place[1:2], none))
         rk[2:3, s] = jnp.where(lv, jnp.where(mv, place[2:3], none), none)
         rk[3:4, s] = jnp.where(lv, place[0:1], none)
     n_b = carry[1:2, 0:1] + 1.0
+    n_c = carry[3:4, 0:1] + 1.0
 
     def one_hot(row, base):
         for k in range(ROWS // 256):
@@ -154,8 +159,12 @@
             c.wait()
         base = slots[p]
         total = accs[p] + arl[base]
+        most = jnp.maximum(accs[p], arl[base])
         if len(phases[p]) == 3:
             total = total + (arl[base + 1] + arl[base + 2])
+            most = jnp.maximum(most, jnp.maximum(arl[base + 1], arl[base + 2]))
+        is_max = lax.broadcasted_iota(jnp.int32, total.shape, 1) >= WIDTH + 64
+        total = jnp.where(is_max, most, total)
         if p < LAST:
             accs[p + 1] = total
         else:
@@ -170,7 +179,7 @@
 
     def c_copy(j, count=CHUNK):
         src = HEAD + j * CHUNK
-        return rows_copy(4 + j, src, held, ROWS + src, count, x2)
+        return rows_copy(4 + j, src, cland, src, count, x2)
 
     def b_copy(j):
         return rows_copy(2 * j, B_AT + j * CHUNK, held, ROWS + CAP_ONE + j * CHUNK, CHUNK, x1)
@@ -178,8 +187,9 @@
     def d_copy(j):
         return rows_copy(2 * j + 1, D_AT + j * CHUNK, dland, j * CHUNK, CHUNK, x3)
 
-    head_copy = rows_copy(4 + C_CHUNKS, 0, held, ROWS, HEAD, x2)
-    last_copy = c_copy(MID, CAP_ONE - HEAD - MID * CHUNK)
+    head_copy = rows_copy(4 + C_CHUNKS, 0, cland, 0, HEAD, x2)
+    late_copy = c_copy(MID, SPLIT - LATE)
+    last_copy = rows_copy(4 + MID + 1, SPLIT, cland, SPLIT, MOST - SPLIT, x2)
     head_copy.start()
 
     def compact(row, base, to):
@@ -199,7 +209,8 @@
         res = res + jnp.dot(both, xv[pl.ds(k * PIECE, PIECE), :], preferred_element_type=F32)
     ybuf[HEAD : HEAD + CHUNK, :] = res[0:CHUNK].astype(BF16)
     accs[0, :, 0:WIDTH] = res[CHUNK : CHUNK + 4]
-    accs[0, :, WIDTH:] = jnp.broadcast_to(count, (4, 128))
+    is_max = lax.broadcasted_iota(jnp.int32, (4, WIDTH + 128), 1) >= WIDTH + 64
+    accs[0, :, WIDTH:] = jnp.where(is_max[:, WIDTH:], n_c, count)
     ar_start(0)
     c_copy(0).start()
 
@@ -238,6 +249,29 @@
         return 0
 
     lax.fori_loop(1, MID, early_c, 0)
+
+    def pack_margins(row, base):
+        one_hot(row, base)
+        return lax.dot_general(
+            vmat[...], lhs[0:CHUNK, :], (((1,), (1,)), ((), ())), preferred_element_type=F32
+        )
+
+    slot = rk[3:4, :]
+    high = slot // 256
+    vmat[...] = stack_rows([high.astype(F32), (slot - 256 * high).astype(F32)], 16).astype(BF16)
+
+    def pack_slots(j, _):
+        r = pack_margins(0, CHUNK * j)
+        s = pl.ds(pl.multiple_of(j * CHUNK, CHUNK), CHUNK)
+        reached = lax.broadcasted_iota(jnp.int32, (1, CHUNK), 1) + CHUNK * j < n_c.astype(jnp.int32)
+        ms_s[0:1, s] = jnp.where(reached, 256.0 * r[0:1] + r[1:2], -1.0)
+        return 0
+
+    lax.fori_loop(0, 8, pack_slots, 0)
+    slot_copy = pltpu.make_async_remote_copy(
+        src_ref=ms_s, dst_ref=slots_out, send_sem=m_send.at[3], recv_sem=m_recv.at[3], device_id=(x2,), device_id_type=MESH,
+    )
+    slot_copy.start()
 
     tot = acc[:, 0:WIDTH]
     num = acc[:, WIDTH : WIDTH + 1]
@@ -245,6 +279,7 @@
     pair_sum = jnp.concatenate([tot[0:1] + tot[1:2], tot[2:3] + tot[3:4]], axis=0)
     pair_num = jnp.concatenate([num[0:1] + num[1:2], num[2:3] + num[3:4]], axis=0)
     c1 = pair_sum / pair_num
+    flag[...] = jnp.broadcast_to(acc[0:1, WIDTH + 64 : WIDTH + 65], (8, 128))
     cent[0:2, :] = c1
     cent[2:6, :] = c2
     six = jnp.concatenate([c1, c2, jnp.zeros((2, WIDTH), F32)], axis=0)
@@ -269,12 +304,6 @@
         return 0
 
     lax.fori_loop(0, 8, margins, 0)
-
-    def pack_margins(row, base):
-        one_hot(row, base)
-        return lax.dot_general(
-            vmat[...], lhs[0:CHUNK, :], (((1,), (1,)), ((), ())), preferred_element_type=F32
-        )
 
     def pack_c(j, _):
         r = pack_margins(3, CHUNK * j)
@@ -317,7 +346,10 @@
         return 0
 
     lax.fori_loop(MID, C_CHUNKS, late, 0)
+    late_copy.start()
     last_copy.start()
+    spare = pltpu.make_async_copy(ybuf.at[pl.ds(MOST, CAP_ONE - MOST)], rest, load_sem.at[0])
+    spare.start()
 
     def keep(k, _):
         s = pl.ds(pl.multiple_of(k * 256, 256), 256)
@@ -369,10 +401,53 @@
     head_copy.wait()
     for j in range(MID):
         c_copy(j).wait()
+    slot_copy.wait()
+    slot_store = pltpu.make_async_copy(slots_out, slots_hbm, load_sem.at[1])
+    slot_store.start()
+
+    def spread(k, at, size):
+        slot = lax.broadcasted_iota(jnp.int32, (CHUNK, size), 0) + k * CHUNK
+        hot = jnp.where(slot == slots_out[0:1, at : at + size].astype(jnp.int32), 1.0, 0.0).astype(BF16)
+        return jnp.dot(hot, cland[at : at + size, :], preferred_element_type=F32)
+
+    def spread_first(k, _):
+        s = pl.ds(pl.multiple_of(ROWS + k * CHUNK, CHUNK), CHUNK)
+        held[s, :] = spread(k, 0, LATE).astype(BF16)
+        return 0
+
+    lax.fori_loop(0, CAP_ONE // CHUNK, spread_first, 0)
+
+    def spread_more(at, size):
+        def body(k, _):
+            s = pl.ds(pl.multiple_of(ROWS + k * CHUNK, CHUNK), CHUNK)
+            held[s, :] = (held[s, :].astype(F32) + spread(k, at, size)).astype(BF16)
+            return 0
+
+        lax.fori_loop(at // CHUNK, CAP_ONE // CHUNK, body, 0)
+
+    spare.wait()
+    slot_store.wait()
+    late_copy.wait()
+    spread_more(LATE, SPLIT - LATE)
     last_copy.wait()
+    spread_more(SPLIT, MOST - SPLIT)
+
+
+def rest_kernel(rest, extra, send_sem, recv_sem):
+    me = lax.axis_index("cube")
+    other = me + 64 - 128 * (me // 64)
+    barrier = pltpu.get_barrier_semaphore()
+    pl.semaphore_signal(barrier, inc=1, device_id=(other,), device_id_type=MESH)
+    pl.semaphore_wait(barrier, 1)
+    copy = pltpu.make_async_remote_copy(
+        src_ref=rest, dst_ref=extra, send_sem=send_sem, recv_sem=recv_sem, device_id=(other,), device_id_type=MESH
+    )
+    copy.start()
+    copy.wait()
 
 
 PIECES = 14
+END = ROWS + CAP_ONE - CHUNK
 
 
 def store_kernel(held, m1, m2, cent, held_out, m1_out, m2_out, cent_out, sem):
@@ -389,20 +464,40 @@
         c.wait()
 
 
+def add_kernel(held, slots, extra, held_out, rows, sem):
+    load = pltpu.make_async_copy(held.at[pl.ds(END, CHUNK)], rows, sem)
+    load.start()
+    load.wait()
+    slot = lax.broadcasted_iota(jnp.int32, (CHUNK, CAP_ONE - MOST), 0) + CAP_ONE - CHUNK
+    hot = jnp.where(slot == slots[0:1, MOST:CAP_ONE].astype(jnp.int32), 1.0, 0.0).astype(BF16)
+    more = jnp.dot(hot, extra[...], preferred_element_type=F32)
+    rows[...] = (rows[...].astype(F32) + more).astype(BF16)
+    back = pltpu.make_async_copy(rows, held_out.at[pl.ds(END, CHUNK)], sem)
+    back.start()
+    back.wait()
+
+
 def local(vectors, child_labels):
     in_vmem = pl.BlockSpec(memory_space=pltpu.VMEM)
     anywhere = pl.BlockSpec(memory_space=pl.ANY)
     shapes = [((HELD, WIDTH), BF16), ((1, ROWS + CAP_ONE), F32), ((1, HELD), F32), ((6, WIDTH), F32)]
     dma = pltpu.SemaphoreType.DMA
-    parts = pl.pallas_call(
+    held_shape = jax.ShapeDtypeStruct((HELD, WIDTH), BF16)
+    rest_shape = jax.ShapeDtypeStruct((CAP_ONE - MOST, WIDTH), BF16)
+    *parts, flag, rest, slots = pl.pallas_call(
         exchange_kernel,
-        out_shape=tuple(pltpu.VMEM(s, d) for s, d in shapes),
+        out_shape=(
+            *(pltpu.VMEM(s, d) for s, d in shapes + [((8, 128), F32)]),
+            rest_shape,
+            jax.ShapeDtypeStruct((1, CAP_ONE), F32),
+        ),
         in_specs=[anywhere, anywhere],
-        out_specs=(in_vmem,) * 4,
+        out_specs=(in_vmem,) * 5 + (anywhere,) * 2,
         scratch_shapes=[
             pltpu.VMEM((ROWS, WIDTH), BF16),
             pltpu.VMEM((2, ROWS), jnp.int32),
             pltpu.VMEM((PACKED, WIDTH), BF16),
+            pltpu.VMEM((MOST, WIDTH), BF16),
             pltpu.VMEM((HALF, WIDTH), BF16),
             pltpu.VMEM((CHUNK, ROWS), BF16),
             pltpu.VMEM((8, ROWS), jnp.int32),
@@ -413,6 +508,8 @@
             pltpu.VMEM((2, CAP_ONE), F32),
             pltpu.VMEM((2, HALF), F32),
             pltpu.VMEM((2, HALF), F32),
+            pltpu.VMEM((1, CAP_ONE), F32),
+            pltpu.VMEM((1, CAP_ONE), F32),
             pltpu.VMEM((2, CAP_ONE), F32),
             pltpu.VMEM((2, HALF), F32),
             pltpu.VMEM((2, HALF), F32),
@@ -421,14 +518,23 @@
             dma((8,)),
             dma((C_CHUNKS + 5,)),
             dma((C_CHUNKS + 5,)),
-            dma((3,)),
-            dma((3,)),
+            dma((4,)),
+            dma((4,)),
         ],
         compiler_params=pltpu.CompilerParams(
             collective_id=0, has_side_effects=True, vmem_limit_bytes=44 << 20
         ),
         name="exchange",
     )(vectors, child_labels)
+    send_rest = pl.pallas_call(
+        rest_kernel,
+        out_shape=rest_shape,
+        in_specs=[anywhere],
+        out_specs=anywhere,
+        scratch_shapes=[dma, dma],
+        compiler_params=pltpu.CompilerParams(collective_id=1, has_side_effects=True),
+        name="rest",
+    )
     held, m1, m2, cent = pl.pallas_call(
         store_kernel,
         out_shape=tuple(jax.ShapeDtypeStruct(s, d) for s, d in shapes),
@@ -438,6 +544,24 @@
         compiler_params=pltpu.CompilerParams(vmem_limit_bytes=16 << 20),
         name="store",
     )(*parts)
+    add_rest = pl.pallas_call(
+        add_kernel,
+        out_shape=held_shape,
+        in_specs=[anywhere, in_vmem, in_vmem],
+        out_specs=anywhere,
+        scratch_shapes=[pltpu.VMEM((CHUNK, WIDTH), BF16), dma],
+        input_output_aliases={0: 0},
+        compiler_params=pltpu.CompilerParams(vmem_limit_bytes=16 << 20),
+        name="add",
+    )
+
+    steps = (flag[0, 0] > MOST).astype(jnp.int32)
+
+    def step(carry):
+        done, rows = carry
+        return done + 1, add_rest(rows, slots, send_rest(rest))
+
+    _, held = lax.while_loop(lambda carry: carry[0] < steps, step, (jnp.int32(0), held))
     return held, m1.reshape(-1), m2.reshape(-1), cent
 
 

time: 98.6 us -> 92 us (0.933)
  Pallas kernels: 97.8 us -> 89.8 us
    pallas_call x1, Pallas kernels: 93.6 us -> 85.5 us  [local(): pl.pallas_call(exchange_kernel, out_shape=(*(pltpu.VMEM(s, d) for s, d in...]
where the time goes in v3:
time: 92 us; the launch traced here: 91.8 us
  Pallas kernels  89.8 us (98%)
  between operations  1.46 us (2%)
    pallas_call x1, Pallas kernels, local(): pl.pallas_call(exchange_kernel, out_shape=(*(pltpu.VMEM(s, d) for s, d in...  85.5 us
    pallas_call x1, Pallas kernels, local(): pl.pallas_call(store_kernel, out_shape=tuple((jax.ShapeDtypeStruct(s, d)...  4.25 us

profile of v3, /device:TPU:1, one launch (start us, length us, event | category | flops | bytes accessed | tf_op | source)
XLA Modules:
  0.0 91.8 jit_solution(16466455238806992569)
XLA Ops:
  0.6 85.5 %exchange.1 = (bf16[7168,768]{1,0:T(8,128)(2,1)S(1)}, f32[1,6144]{1,0:T(1,128)S(1)}, f32[1,7168]{1,0:T(1,128)S(1)}, f32[6,768]{1,0:T(8,128)S(1)}, f32[8,128]{1,0...) custom-call(bf16[4096,768]{1,0:T(8,128)(2,1)} %x_ref.1, s32[2,4096]{1,0:T(2,128)} %lab_any.1), custom_call_target="tpu_custom_call" | custom-call | tf_op jit(solution)/shard_map/exchange/pallas_call | solution.py:487
  86.2 0.5 slice.3
  87.3 4.2 %store.1 = (bf16[7168,768]{1,0:T(8,128)(2,1)}, f32[1,6144]{1,0:T(1,128)}, f32[1,7168]{1,0:T(1,128)}, f32[6,768]{1,0:T(8,128)}) custom-call(bf16[7168,768]{1,0:T(8,128)(2,1)S(1)} %get-tuple-element.43.held, f32[1,6144]{1,0:T(1,128)S(1)} %get-tuple-element.44.m1, f32[1,7168]{1,0:T(1,128)S(1)} %get-tuple-element.45.m2, f32[6,768]{1,0:T(8,128)S(1)} %get-tuple-element.46.cent), custom_call_target="tpu_custom_call" | custom-call | tf_op jit(solution)/shard_map/store/pallas_call | solution.py:538
  (1 shorter events, 0.0 us)

commit v4 on v3

--- a/solution.py
+++ b/solution.py
@@ -279,7 +279,7 @@
     pair_sum = jnp.concatenate([tot[0:1] + tot[1:2], tot[2:3] + tot[3:4]], axis=0)
     pair_num = jnp.concatenate([num[0:1] + num[1:2], num[2:3] + num[3:4]], axis=0)
     c1 = pair_sum / pair_num
-    flag[...] = jnp.broadcast_to(acc[0:1, WIDTH + 64 : WIDTH + 65], (8, 128))
+    flag[...] = jnp.where(acc[0:1, WIDTH + 64 : WIDTH + 65] > MOST, 1, 0)
     cent[0:2, :] = c1
     cent[2:6, :] = c2
     six = jnp.concatenate([c1, c2, jnp.zeros((2, WIDTH), F32)], axis=0)
@@ -487,7 +487,7 @@
     *parts, flag, rest, slots = pl.pallas_call(
         exchange_kernel,
         out_shape=(
-            *(pltpu.VMEM(s, d) for s, d in shapes + [((8, 128), F32)]),
+            *(pltpu.VMEM(s, d) for s, d in shapes + [((1, 1), jnp.int32)]),
             rest_shape,
             jax.ShapeDtypeStruct((1, CAP_ONE), F32),
         ),
@@ -555,7 +555,7 @@
         name="add",
     )
 
-    steps = (flag[0, 0] > MOST).astype(jnp.int32)
+    steps = flag.reshape(())
 
     def step(carry):
         done, rows = carry

time: 92 us -> 91.8 us (level)
  no operation moved by 1% of the time
where the time goes in v4:
time: 91.8 us; the launch traced here: 91.6 us
  Pallas kernels  90.1 us (98%)
    pallas_call x1, Pallas kernels, local(): pl.pallas_call(exchange_kernel, out_shape=(*(pltpu.VMEM(s, d) for s, d in...  85.9 us
    pallas_call x1, Pallas kernels, local(): pl.pallas_call(store_kernel, out_shape=tuple((jax.ShapeDtypeStruct(s, d)...  4.25 us

profile of v4, /device:TPU:1, one launch (start us, length us, event | category | flops | bytes accessed | tf_op | source)
XLA Modules:
  0.0 91.6 jit_solution(1437627764400756989)
XLA Ops:
  0.6 85.9 %exchange.1 = (bf16[7168,768]{1,0:T(8,128)(2,1)S(1)}, f32[1,6144]{1,0:T(1,128)S(1)}, f32[1,7168]{1,0:T(1,128)S(1)}, f32[6,768]{1,0:T(8,128)S(1)}, s32[1,1]{1,0:T...) custom-call(bf16[4096,768]{1,0:T(8,128)(2,1)} %x_ref.1, s32[2,4096]{1,0:T(2,128)} %lab_any.1), custom_call_target="tpu_custom_call" | custom-call | tf_op jit(solution)/shard_map/exchange/pallas_call | solution.py:487
  86.5 4.2 %store.1 = (bf16[7168,768]{1,0:T(8,128)(2,1)}, f32[1,6144]{1,0:T(1,128)}, f32[1,7168]{1,0:T(1,128)}, f32[6,768]{1,0:T(8,128)}) custom-call(bf16[7168,768]{1,0:T(8,128)(2,1)S(1)} %get-tuple-element.43.held, f32[1,6144]{1,0:T(1,128)S(1)} %get-tuple-element.44.m1, f32[1,7168]{1,0:T(1,128)S(1)} %get-tuple-element.45.m2, f32[6,768]{1,0:T(8,128)S(1)} %get-tuple-element.46.cent), custom_call_target="tpu_custom_call" | custom-call | tf_op jit(solution)/shard_map/store/pallas_call | solution.py:538
  90.8 0.7 while.10
